TPU v7x, 32 devices: a whole 2x2x4 slice. The times are simulated.
32 devices in a mesh: dp: 4 (over z), ctx: 4 (over x, core), tp: 2 (over y).
Axes of the slice: x: 2, y: 2, z: 4, core: 2. Of those that a mesh axis runs over, the one named last changes fastest.
Arguments:
- projected: bfloat16 [4, 3, 4096, 1024], P('dp', None, 'tp', 'ctx'), may hold values from -6 to 6
- cotangent: bfloat16 [4, 4096, 1024], P('dp', None, ('ctx', 'tp')), may hold values from -6 to 6
- short_filter: float32 [3, 3, 4096], P(None, None, 'tp'), may hold values from -3 to 3
- residues: float32 [4096, 16], P('tp'), may hold values from -3 to 3
- decay_rate: float32 [4096, 16], P('tp'), may hold values from 0.00024414062 to 0.035
- skip_gain: float32 [4096], P('tp'), may hold values from -1 to 1
Outputs:
- hyena_out: bfloat16 [4, 4096, 1024], P('dp', 'tp', 'ctx')
- input_grad: bfloat16 [4, 3, 4096, 1024], P('dp', None, 'tp', 'ctx')
- residue_grad: float32 [4096, 16], P('tp')
- skip_grad: float32 [4096], P('tp')
All inputs are finite; a program needn't handle non-finite values.
Results may differ from a plain program's by a relative error of at most 0.0076.
Values may be sent and summed in bfloat16 or wider, within the bound.
A program may use at most 128 MiB of HBM per device.

v0:
```python
import math

import jax
import jax.numpy as jnp
from jax import lax
from jax.experimental import pallas as pl
from jax.experimental.pallas import tpu as pltpu
from jax.sharding import PartitionSpec as P

LANES = 128
SUBS = 8
F32 = jnp.float32
BF16 = jnp.bfloat16


def rounded(values):
    return values.astype(BF16).astype(F32)


def nt_dot(left, right):
    return lax.dot_general(left, right, (((1,), (1,)), ((), ())), preferred_element_type=F32)


def row_of(ref, index):
    return jnp.broadcast_to(ref[index : index + 1, :], (SUBS, LANES))


def tree_sum(terms):
    terms = list(terms)
    while len(terms) > 1:
        paired = [terms[i] + terms[i + 1] for i in range(0, len(terms) - 1, 2)]
        if len(terms) % 2:
            paired.append(terms[-1])
        terms = paired
    return terms[0]


def sublane_ids():
    return lax.broadcasted_iota(jnp.int32, (SUBS, LANES), 0)


def scan_subs(ends, rate, span, sub, backward):
    running = ends
    step = 1
    while step < SUBS:
        if backward:
            moved = jnp.where(sub < SUBS - step, pltpu.roll(running, SUBS - step, 0), 0.0)
        else:
            moved = jnp.where(sub >= step, pltpu.roll(running, step, 0), 0.0)
        running = running + jnp.exp(-rate * float(span * step)) * moved
        step *= 2
    if backward:
        before = jnp.where(sub < SUBS - 1, pltpu.roll(running, SUBS - 1, 0), 0.0)
    else:
        before = jnp.where(sub >= 1, pltpu.roll(running, 1, 0), 0.0)
    return before, running


def first_kernel(proj, cot, rim, taps, rate, perm, feat, inner, totals, edge, u_s, d_s):
    order = rate.shape[0]
    tokens = proj.shape[2]
    span = tokens // SUBS
    sub = sublane_ids()
    streams = []
    for s in range(3):
        rows = nt_dot(perm[...], proj[s])
        last = jnp.where(
            sub == 0, row_of(rim, 2 * s + 1), pltpu.roll(rows[tokens - SUBS :], 1, 0)
        )
        prior = jnp.where(
            sub == 0,
            row_of(rim, 2 * s),
            pltpu.roll(rows[tokens - 2 * SUBS : tokens - SUBS], 1, 0),
        )
        wide = jnp.concatenate([prior, last, rows], axis=0)
        made = taps[3 * s : 3 * s + 1, :] * rows
        made = made + taps[3 * s + 1 : 3 * s + 2, :] * wide[SUBS : SUBS + tokens]
        made = made + taps[3 * s + 2 : 3 * s + 3, :] * wide[:tokens]
        narrow = made.astype(BF16)
        feat[s] = narrow
        streams.append(narrow.astype(F32))
    pieces, part = cot.shape[0], cot.shape[2]
    grad = nt_dot(perm[:, :part], cot[0])
    for p in range(1, pieces):
        grad = grad + nt_dot(perm[:, p * part : (p + 1) * part], cot[p])
    feat[3] = grad.astype(BF16)
    streams.append(grad)
    for s in range(4):
        edge[2 * s : 2 * s + 1, :] = streams[s][0:1]
        edge[2 * s + 1 : 2 * s + 2, :] = streams[s][SUBS : SUBS + 1]
    u_s[...] = rounded(streams[1] * streams[2])
    d_s[...] = rounded(streams[3] * streams[0])
    falls = [jnp.exp(-row_of(rate, n)) for n in range(order)]

    def body(j, carry):
        ahead, back = carry
        uj = u_s[pl.ds(pl.multiple_of(j * SUBS, SUBS), SUBS), :]
        dj = d_s[pl.ds(pl.multiple_of((span - 1 - j) * SUBS, SUBS), SUBS), :]
        ahead = tuple(falls[n] * ahead[n] + uj for n in range(order))
        back = tuple(falls[n] * back[n] + dj for n in range(order))
        return ahead, back

    zero = jnp.zeros((SUBS, LANES), F32)
    ahead, back = lax.fori_loop(0, span, body, ((zero,) * order, (zero,) * order), unroll=4)
    for n in range(order):
        rate_n = row_of(rate, n)
        before, running = scan_subs(ahead[n], rate_n, span, sub, False)
        inner[n * SUBS : (n + 1) * SUBS, :] = before
        totals[n : n + 1, :] = running[SUBS - 1 : SUBS]
        before, running = scan_subs(back[n], rate_n, span, sub, True)
        inner[(order + n) * SUBS : (order + n + 1) * SUBS, :] = before
        totals[order + n : order + n + 1, :] = running[0:1]


def second_kernel(
    scale, feat, inner, states, edge, taps, rate, res, gain, perm_t, ident,
    out, grad_in, sums, u_s, d_s, z_s, b_s, a_s, w_s, x_s,
):
    order = rate.shape[0]
    tokens = feat.shape[1]
    span = tokens // SUBS
    sub = sublane_ids()
    sub_f = sub.astype(F32)
    root = jnp.sqrt(2.0 * rate[...])
    weight = res[...] * root
    fall = jnp.exp(-rate[...])
    for n in range(order):
        a_s[n * SUBS : (n + 1) * SUBS, :] = jnp.broadcast_to(fall[n : n + 1], (SUBS, LANES))
        w_s[n * SUBS : (n + 1) * SUBS, :] = jnp.broadcast_to(weight[n : n + 1], (SUBS, LANES))
    gain_b = jnp.broadcast_to(gain[...], (SUBS, LANES))
    u_s[...] = rounded(feat[1].astype(F32) * feat[2].astype(F32))
    d_s[...] = rounded(feat[3].astype(F32) * feat[0].astype(F32))

    def mode(ref, n):
        return ref[n * SUBS : (n + 1) * SUBS, :]

    def ahead_body(j, carry):
        xs, gs, skip = carry
        at = pl.ds(pl.multiple_of(j * SUBS, SUBS), SUBS)
        uj, dj = u_s[at, :], d_s[at, :]
        xs = tuple(mode(a_s, n) * xs[n] + uj for n in range(order))
        gs = tuple(gs[n] + dj * xs[n] for n in range(order))
        y = tree_sum([mode(w_s, n) * xs[n] for n in range(order)])
        z_s[at, :] = rounded(y + gain_b * uj)
        return xs, gs, skip + dj * uj

    zero = jnp.zeros((SUBS, LANES), F32)
    start = tuple(
        mode(inner, n) + jnp.exp(-row_of(rate, n) * (sub_f * float(span))) * row_of(states, n)
        for n in range(order)
    )
    xs, gs, skip = lax.fori_loop(
        0, span, ahead_body, (start, (zero,) * order, zero), unroll=4
    )
    for n in range(order):
        sums[n : n + 1, :] = jnp.sum(gs[n], axis=0, keepdims=True)
        x_s[n : n + 1, :] = xs[n][SUBS - 1 : SUBS]
    sums[0:order, :] = sums[0:order, :] * root * scale
    sums[order : order + SUBS, :] = jnp.broadcast_to(
        jnp.sum(skip, axis=0, keepdims=True) * scale, (SUBS, LANES)
    )

    def back_body(i, xs):
        at = pl.ds(pl.multiple_of((span - 1 - i) * SUBS, SUBS), SUBS)
        dj = d_s[at, :]
        xs = tuple(mode(a_s, n) * xs[n] + dj for n in range(order))
        y = tree_sum([mode(w_s, n) * xs[n] for n in range(order)])
        b_s[at, :] = rounded(y + gain_b * dj)
        return xs

    start = tuple(
        mode(inner, order + n)
        + jnp.exp(-row_of(rate, n) * ((SUBS - 1.0 - sub_f) * float(span)))
        * row_of(states, order + n)
        for n in range(order)
    )
    lax.fori_loop(0, span, back_body, start, unroll=4)

    gain_r = gain[...]
    q_n, k_n, v_n, g_n = (
        [edge[2 * s : 2 * s + 1, :], edge[2 * s + 1 : 2 * s + 2, :]] for s in range(4)
    )
    u_n = [rounded(k_n[i] * v_n[i]) for i in range(2)]
    d_n = [rounded(g_n[i] * q_n[i]) for i in range(2)]
    state = x_s[...]
    b_state = states[order : 2 * order, :]
    next_rows = []
    for i in range(2):
        state = fall * state + u_n[i]
        z_n = rounded(jnp.sum(weight * state, axis=0, keepdims=True) + gain_r * u_n[i])
        if i:
            b_state = (b_state - d_n[i - 1]) / fall
        du_n = rounded(jnp.sum(weight * b_state, axis=0, keepdims=True) + gain_r * d_n[i])
        next_rows.append(
            [rounded(g_n[i] * z_n), rounded(du_n * v_n[i]), rounded(du_n * k_n[i])]
        )

    def send_out(rows):
        ordered = jnp.dot(perm_t[...], rows, preferred_element_type=F32).astype(BF16)
        return nt_dot(ident[...], ordered).astype(BF16)

    z = z_s[...]
    du = b_s[...]
    out[...] = send_out((feat[0].astype(F32) * z).astype(BF16))
    for s in range(3):
        if s == 0:
            rows = rounded(feat[3].astype(F32) * z)
        else:
            rows = rounded(du * feat[3 - s].astype(F32))
        after = [
            jnp.where(
                sub == SUBS - 1,
                jnp.broadcast_to(next_rows[i][s], (SUBS, LANES)),
                pltpu.roll(rows[i * SUBS : (i + 1) * SUBS], SUBS - 1, 0),
            )
            for i in range(2)
        ]
        wide = jnp.concatenate([rows] + after, axis=0)
        made = taps[3 * s : 3 * s + 1, :] * rows
        made = made + taps[3 * s + 1 : 3 * s + 2, :] * wide[SUBS : SUBS + tokens]
        made = made + taps[3 * s + 2 : 3 * s + 3, :] * wide[2 * SUBS :]
        grad_in[s] = send_out(made.astype(BF16))


def shifted(array, by):
    count = lax.axis_size("ctx")
    pairs = [(i, i + by) for i in range(count) if 0 <= i + by < count]
    return lax.ppermute(array, "ctx", pairs)


def entering(total, span_rate, first, sign):
    count = lax.axis_size("ctx")
    result, width = first, 1
    window = total + jnp.exp(-span_rate) * first
    reach = 2
    while width < count - 1:
        moved = shifted(window, sign * reach)
        result = result + jnp.exp(-span_rate * float(width)) * moved
        width += reach
        if width < count - 1:
            window = window + jnp.exp(-span_rate * float(reach)) * moved
        reach *= 2
    return result


def on_device(projected, cotangent, short_filter, residues, decay_rate, skip_gain):
    proj = projected[0]
    _, chans, tokens = proj.shape
    order = residues.shape[1]
    span = tokens // SUBS
    tiles = chans // LANES
    pieces = lax.axis_size("tp")
    total_tokens = tokens * lax.axis_size("ctx") * lax.axis_size("dp")
    scale = 1.0 / math.sqrt(total_tokens)

    cot = cotangent[0].reshape(pieces, chans, tokens // pieces)
    cot = lax.all_to_all(cot, "tp", split_axis=0, concat_axis=0, tiled=True)
    rim = jnp.swapaxes(proj[:, :, tokens - 2 :], 1, 2).reshape(6, chans)
    rim = shifted(rim, 1).astype(F32)
    taps = short_filter.reshape(9, chans)
    rate = decay_rate.T
    res = residues.T
    gain = skip_gain[None]
    r = jnp.arange(tokens)
    perm = ((r % SUBS) * span + r // SUBS)[:, None] == r[None, :]
    perm_t = perm.T.astype(BF16)
    perm = perm.astype(BF16)
    ident = jnp.eye(LANES, dtype=BF16)

    def cols(*lead):
        zeros = (0,) * len(lead)
        return pl.BlockSpec(lead + (LANES,), lambda i: zeros + (i,))

    def whole(rows, columns):
        return pl.BlockSpec((rows, columns), lambda i: (0, 0))

    def chan_rows(lead, last):
        return pl.BlockSpec((lead, LANES, last), lambda i: (0, i, 0))

    params = pltpu.CompilerParams(
        dimension_semantics=("arbitrary",), vmem_limit_bytes=40 * 2**20
    )
    work = chans * tokens * order
    feat, inner, totals, edge = pl.pallas_call(
        first_kernel,
        grid=(tiles,),
        in_specs=[
            chan_rows(3, tokens),
            chan_rows(pieces, tokens // pieces),
            cols(6),
            cols(9),
            cols(order),
            whole(tokens, tokens),
        ],
        out_specs=[cols(4, tokens), cols(2 * order * SUBS), cols(2 * order), cols(8)],
        out_shape=[
            jax.ShapeDtypeStruct((4, tokens, chans), BF16),
            jax.ShapeDtypeStruct((2 * order * SUBS, chans), F32),
            jax.ShapeDtypeStruct((2 * order, chans), F32),
            jax.ShapeDtypeStruct((8, chans), F32),
        ],
        scratch_shapes=[pltpu.VMEM((tokens, LANES), F32)] * 2,
        compiler_params=params,
        cost_estimate=pl.CostEstimate(
            flops=4 * work, bytes_accessed=2**23, transcendentals=0
        ),
    )(proj, cot, rim, taps, rate, perm)

    span_rate = rate * float(tokens)
    ahead, back = totals[:order], totals[order:]
    first_ahead = shifted(ahead, 1)
    first_back = shifted(jnp.concatenate([back, edge], axis=0), -1)
    next_edge = first_back[order:]
    states = jnp.concatenate(
        [
            entering(ahead, span_rate, first_ahead, 1),
            entering(back, span_rate, first_back[:order], -1),
        ],
        axis=0,
    )

    out, grad_in, sums = pl.pallas_call(
        lambda *refs: second_kernel(scale, *refs),
        grid=(tiles,),
        in_specs=[
            cols(4, tokens),
            cols(2 * order * SUBS),
            cols(2 * order),
            cols(8),
            cols(9),
            cols(order),
            cols(order),
            cols(1),
            whole(tokens, tokens),
            whole(LANES, LANES),
        ],
        out_specs=[
            pl.BlockSpec((LANES, tokens), lambda i: (i, 0)),
            chan_rows(3, tokens),
            cols(order + SUBS),
        ],
        out_shape=[
            jax.ShapeDtypeStruct((chans, tokens), BF16),
            jax.ShapeDtypeStruct((3, chans, tokens), BF16),
            jax.ShapeDtypeStruct((order + SUBS, chans), F32),
        ],
        scratch_shapes=[pltpu.VMEM((tokens, LANES), F32)] * 4
        + [pltpu.VMEM((order * SUBS, LANES), F32)] * 2
        + [pltpu.VMEM((order, LANES), F32)],
        compiler_params=params,
        cost_estimate=pl.CostEstimate(
            flops=12 * work, bytes_accessed=2**23, transcendentals=0
        ),
    )(feat, inner, states, next_edge, taps, rate, res, gain, perm_t, ident)
    sums = lax.psum(sums, ("dp", "ctx"))
    return (out[None], grad_in[None], sums[:order].T, sums[order])


def solution(mesh):
    placed = (
        P("dp", None, "tp", "ctx"),
        P("dp", None, ("ctx", "tp")),
        P(None, None, "tp"),
        P("tp", None),
        P("tp", None),
        P("tp"),
    )
    return jax.shard_map(
        on_device,
        mesh=mesh,
        in_specs=placed,
        out_specs=(P("dp", "tp", "ctx"), P("dp", None, "tp", "ctx"), P("tp", None), P("tp")),
        check_vma=False,
    )
```

profile of v0, /device:TPU:0, one launch (start us, length us, event | category | flops | bytes accessed | tf_op | source)
XLA Modules:
  0.0 195.8 jit_solution(9437066732975827518)
XLA Ops:
  7.2 4.4 %all-to-all-start = ((bf16[2,2048,128]{2,1,0:T(8,128)(2,1)}), bf16[2,2048,128]{2,1,0:T(8,128)(2,1)}, u32[]{:S(2)}, u32[]{:S(2)}) async-start(bf16[2,2048,128]{2,1,0:T(8,128)(2,1)} %bitcast.22), calls=%async_computation | async-start | bytes 2097152 | tf_op jit(solution)/shard_map/all_to_all | solution.py:257
  11.6 0.0 all-reduce.2.cloned.1.call-start
  11.7 3.2 %slice_bitcast_fusion = bf16[3,2,2048]{1,2,0:T(8,128)(2,1)} fusion(bf16[3,2048,256]{2,1,0:T(8,128)(2,1)} %bitcast.16), kind=kLoop, calls=%fused_computation | loop fusion | bytes 49152 | tf_op jit(solution)/shard_map/transpose | solution.py:258
  14.9 1.7 copy.10
  16.6 0.6 reshape.36
  17.2 2.9 %collective-permute-start = (bf16[6,2048]{1,0:T(8,128)(2,1)}, bf16[6,2048]{1,0:T(8,128)(2,1)}, u32[]{:S(2)}, u32[]{:S(2)}) collective-permute-start(bf16[6,2048]{1,0:T(8,128)(2,1)} %reshape.36), channel_id=1, source_target_pairs={{0,2},{2,4},{4,6},{1,3},{3,5},{5,7},{8,10},{10,12},{12,14},{9,11},... | collective-permute-start | bytes 73736 | tf_op jit(solution)/shard_map/ppermute | solution.py:228
  20.2 0.8 fusion.1
  20.9 0.9 reshape.37.taps.refs_4_
  21.9 1.4 convert_element_type.12.rim
  23.3 3.5 %all-to-all-done.cot = bf16[2,2048,128]{2,1,0:T(8,128)(2,1)} async-done(((bf16[2,2048,128]{2,1,0:T(8,128)(2,1)}), bf16[2,2048,128]{2,1,0:T(8,128)(2,1)}, u32[]{:S(2)}, u32[]{:S(2)}) %all-to-all-start) | async-done | bytes 1048608 | tf_op jit(solution)/shard_map/all_to_all | solution.py:257
  26.8 0.9 copy-done.2
  27.7 0.8 copy-done.3
  28.5 14.8 %shard_map.93 = (bf16[4,256,2048]{2,1,0:T(8,128)(2,1)S(1)}, f32[256,2048]{1,0:T(8,128)S(1)}, f32[32,2048]{1,0:T(8,128)S(1)}, f32[8,2048]{1,0:T(8,128)S(1)}) custom-call(bf16[3,2048,256]{2,1,0:T(8,128)(2,1)S(1)} %bitcast.17, bf16[2,2048,128]{2,1,0:T(8,128)(2,1)} %all-to-all-done.cot, f32[6,2048]{1,0:T(8,128)S(1)} %copy-done.3, ...), custom_call_target="tpu_custom_call" | custom-call | flops 33554432 | bytes 8388608 | tf_op jit(solution)/shard_map/pallas_call | solution.py:284
  43.4 1.3 collective-permute-start.3
  44.7 3.0 %collective-permute-start.1 = (f32[16,2048]{1,0:T(8,128)S(1)}, f32[16,2048]{1,0:T(8,128)S(1)}, u32[]{:S(2)}, u32[]{:S(2)}) collective-permute-start(f32[16,2048]{1,0:T(8,128)S(1)} %get-tuple-element.20), channel_id=1, source_target_pairs={{0,2},{2,4},{4,6},{1,3},{3,5},{5,7},{8,10},{10,12},{12,14},{9,11},... | collective-permute-start | bytes 393224 | tf_op jit(solution)/shard_map/ppermute | solution.py:228
  47.8 1.0 collective-permute-done.1
  48.8 6.5 %collective-permute-start.2 = (f32[16,2048]{1,0:T(8,128)S(1)}, f32[16,2048]{1,0:T(8,128)S(1)}, u32[]{:S(2)}, u32[]{:S(2)}) collective-permute-start(f32[16,2048]{1,0:T(8,128)S(1)} %get-tuple-element.18), channel_id=1, source_target_pairs={{0,4},{2,6},{1,5},{3,7},{8,12},{10,14},{9,13},{11,15},{16,20},{18,... | collective-permute-start | bytes 393224 | tf_op jit(solution)/shard_map/ppermute | solution.py:228
  55.3 1.3 collective-permute-start.4
  56.7 1.2 collective-permute-done.2
  57.8 4.4 %collective-permute-done.4 = f32[16,2048]{1,0:T(8,128)S(1)} collective-permute-done((f32[16,2048]{1,0:T(8,128)S(1)}, f32[16,2048]{1,0:T(8,128)S(1)}, u32[]{:S(2)}, u32[]{:S(2)}) %collective-permute-start.4) | collective-permute-done | bytes 131104 | tf_op jit(solution)/shard_map/ppermute | solution.py:228
  62.3 34.5 %shard_map.94 = (bf16[2048,256]{1,0:T(8,128)(2,1)}, bf16[3,2048,256]{2,1,0:T(8,128)(2,1)}, f32[24,2048]{1,0:T(8,128)}) custom-call(bf16[4,256,2048]{2,1,0:T(8,128)(2,1)S(1)} %get-tuple-element.11.refs_0_, f32[256,2048]{1,0:T(8,128)S(1)} %get-tuple-element.12.refs_1_, f32[32,2048]{1,0:T(8,128)S(1)} %pad_maximum_fusion.refs_2_, f32[8,2048]{1,0:T(8,128)S(1)} %slice.30.refs_3_, ...), custom_call_target="tpu_custom_call" | custom-call | flops 100663296 | bytes 8388608 | tf_op jit(solution)/shard_map/pallas_call | solution.py:322
  96.9 89.1 %all-reduce.2.cloned.1.call-done = f32[24,2048]{1,0:T(8,128)} async-done(((f32[24,2048]{1,0:T(8,128)}), f32[24,2048]{1,0:T(8,128)}) %all-reduce.2.cloned.1.call-update) | async-done | bytes 196624 | tf_op jit(solution)/shard_map/psum | solution.py:355
  185.9 1.4 slice.32
  187.4 1.6 slice_bitcast_fusion.1
  (21 shorter events, 0.2 us)
Async XLA Ops:
  7.2 19.6 %all-to-all-start = ((bf16[2,2048,128]{2,1,0:T(8,128)(2,1)}), bf16[2,2048,128]{2,1,0:T(8,128)(2,1)}, u32[]{:S(2)}, u32[]{:S(2)}) async-start(bf16[2,2048,128]{2,1,0:T(8,128)(2,1)} %bitcast.22), calls=%async_computation | async-start | bytes 2097152 | tf_op jit(solution)/shard_map/all_to_all | solution.py:257
  11.6 15.2 %copy-start = (bf16[1,3,2048,256]{3,2,1,0:T(8,128)(2,1)S(1)}, bf16[1,3,2048,256]{3,2,1,0:T(8,128)(2,1)}, u32[]{:S(2)}) copy-start(bf16[1,3,2048,256]{3,2,1,0:T(8,128)(2,1)} %param.6) | copy-start | bytes 9437188
  11.6 15.2 %copy-start.1 = (f32[2048,16]{0,1:T(8,128)S(1)}, f32[2048,16]{0,1:T(8,128)}, u32[]{:S(2)}) copy-start(f32[2048,16]{0,1:T(8,128)} %param.10) | copy-start | bytes 393220
  11.6 174.3 %all-reduce.2.cloned.1.call-start = ((), (), s32[]{:S(2)}) async-start(), calls=%async_computation.1 | async-start | bytes 393216 | tf_op jit(solution)/shard_map/psum | solution.py:355
  17.2 4.6 %collective-permute-start = (bf16[6,2048]{1,0:T(8,128)(2,1)}, bf16[6,2048]{1,0:T(8,128)(2,1)}, u32[]{:S(2)}, u32[]{:S(2)}) collective-permute-start(bf16[6,2048]{1,0:T(8,128)(2,1)} %reshape.36), channel_id=1, source_target_pairs={{0,2},{2,4},{4,6},{1,3},{3,5},{5,7},{8,10},{10,12},{12,14},{9,11},... | collective-permute-start | bytes 73736 | tf_op jit(solution)/shard_map/ppermute | solution.py:228
  26.8 0.9 copy-start.2
  27.7 0.8 copy-start.3
  28.5 33.7 %copy-start.4 = (f32[2048,16]{0,1:T(8,128)S(1)}, f32[2048,16]{0,1:T(8,128)}, u32[]{:S(2)}) copy-start(f32[2048,16]{0,1:T(8,128)} %param.9) | copy-start | bytes 393220
  28.5 33.8 %copy-start.5 = (f32[2048]{0:T(1024)S(1)}, f32[2048]{0:T(1024)}, u32[]{:S(2)}) copy-start(f32[2048]{0:T(1024)} %param.11) | copy-start | bytes 24580
  43.4 5.3 %collective-permute-start.3 = (f32[24,2048]{1,0:T(8,128)S(1)}, f32[24,2048]{1,0:T(8,128)S(1)}, u32[]{:S(2)}, u32[]{:S(2)}) collective-permute-start(f32[24,2048]{1,0:T(8,128)S(1)} %pad_maximum_fusion.1), channel_id=1, source_target_pairs={{2,0},{4,2},{6,4},{3,1},{5,3},{7,5},{10,8},{12,10},{14,12},{11,9},... | collective-permute-start | bytes 589832 | tf_op jit(solution)/shard_map/ppermute | solution.py:228
  44.7 4.0 %collective-permute-start.1 = (f32[16,2048]{1,0:T(8,128)S(1)}, f32[16,2048]{1,0:T(8,128)S(1)}, u32[]{:S(2)}, u32[]{:S(2)}) collective-permute-start(f32[16,2048]{1,0:T(8,128)S(1)} %get-tuple-element.20), channel_id=1, source_target_pairs={{0,2},{2,4},{4,6},{1,3},{3,5},{5,7},{8,10},{10,12},{12,14},{9,11},... | collective-permute-start | bytes 393224 | tf_op jit(solution)/shard_map/ppermute | solution.py:228
  48.8 9.0 %collective-permute-start.2 = (f32[16,2048]{1,0:T(8,128)S(1)}, f32[16,2048]{1,0:T(8,128)S(1)}, u32[]{:S(2)}, u32[]{:S(2)}) collective-permute-start(f32[16,2048]{1,0:T(8,128)S(1)} %get-tuple-element.18), channel_id=1, source_target_pairs={{0,4},{2,6},{1,5},{3,7},{8,12},{10,14},{9,13},{11,15},{16,20},{18,... | collective-permute-start | bytes 393224 | tf_op jit(solution)/shard_map/ppermute | solution.py:228
  55.3 6.9 %collective-permute-start.4 = (f32[16,2048]{1,0:T(8,128)S(1)}, f32[16,2048]{1,0:T(8,128)S(1)}, u32[]{:S(2)}, u32[]{:S(2)}) collective-permute-start(f32[16,2048]{1,0:T(8,128)S(1)} %get-tuple-element.19), channel_id=1, source_target_pairs={{4,0},{6,2},{5,1},{7,3},{12,8},{14,10},{13,9},{15,11},{20,16},{22,... | collective-permute-start | bytes 393224 | tf_op jit(solution)/shard_map/ppermute | solution.py:228
Sparse Core Ops, SparseCore 0:
  97.0 88.9 all-reduce.1
where the time goes:
time: 197 us; the launch traced here: 196 us
  waiting for transfers between devices  99.1 us (50%)
  Pallas kernels  49.4 us (25%)
  starting transfers between devices  19.6 us (10%)
  between operations  14.2 us (7%)
  local copies, waits for them, and re-layouts  11.3 us (6%)
  other arithmetic  2.3 us (1%)
    psum x1, waiting for transfers between devices, on_device(): sums = lax.psum(sums, ('dp', 'ctx'))  89.1 us
    pallas_call x1, Pallas kernels, on_device(): pl.pallas_call(lambda *refs: second_kernel(scale, *refs), grid=(tiles,),...  34.5 us
    ppermute x5, starting transfers between devices, shifted(): return lax.ppermute(array, 'ctx', pairs)  15.1 us
    pallas_call x1, Pallas kernels, on_device(): pl.pallas_call(first_kernel, grid=(tiles,), in_specs=[chan_rows(3, tokens...  14.8 us
    ppermute x5, waiting for transfers between devices, shifted(): return lax.ppermute(array, 'ctx', pairs)  6.49 us
    transpose x2, local copies, waits for them, and re-layouts, on_device(): rim = jnp.swapaxes(proj[:, :, tokens - 2:], 1, 2).reshape(6, chans)  4.92 us
    all_to_all x1, starting transfers between devices, on_device(): cot = lax.all_to_all(cot, 'tp', split_axis=0, concat_axis=0, tiled=True)  4.43 us
  transfers between devices with their start and end apart: 7, of which 5 were waited for; matrix products, arithmetic and copies ran while one was open for 4% of the time, Pallas kernels for 0%

commit v1 on v0

--- a/solution.py
+++ b/solution.py
@@ -228,19 +228,245 @@
     return lax.ppermute(array, "ctx", pairs)
 
 
-def entering(total, span_rate, first, sign):
+MESH = pl.DeviceIdType.MESH
+
+
+def exchange_kernel(count, totals, edge, rate, states, next_edge, held_a, held_b, held_e,
+                    send_a, send_b, recv_a, recv_b, edge_sem):
+    order = rate.shape[0]
+    me = lax.axis_index("ctx")
+    barrier = pltpu.get_barrier_semaphore()
+
+    def greet(k, _):
+        pl.semaphore_signal(
+            barrier, inc=1, device_id={"ctx": lax.rem(me + k, count)}, device_id_type=MESH
+        )
+        return 0
+
+    lax.fori_loop(1, count, greet, 0)
+    pl.semaphore_wait(barrier, count - 1)
+
+    def later(k):
+        return pltpu.make_async_remote_copy(
+            src_ref=totals.at[pl.ds(0, order)], dst_ref=held_a.at[me],
+            send_sem=send_a.at[k], recv_sem=recv_a.at[me],
+            device_id={"ctx": lax.rem(me + k, count)}, device_id_type=MESH,
+        )
+
+    def earlier(k):
+        return pltpu.make_async_remote_copy(
+            src_ref=totals.at[pl.ds(order, order)], dst_ref=held_b.at[me],
+            send_sem=send_b.at[k], recv_sem=recv_b.at[me],
+            device_id={"ctx": lax.rem(me + count - k, count)}, device_id_type=MESH,
+        )
+
+    def rim():
+        return pltpu.make_async_remote_copy(
+            src_ref=edge, dst_ref=held_e,
+            send_sem=edge_sem.at[0], recv_sem=edge_sem.at[1],
+            device_id={"ctx": lax.rem(me + count - 1, count)}, device_id_type=MESH,
+        )
+
+    @pl.when(me >= 1)
+    def _():
+        rim().start()
+
+    def begin(k, _):
+        @pl.when(me + k < count)
+        def _():
+            later(k).start()
+
+        @pl.when(me >= k)
+        def _():
+            earlier(k).start()
+
+        return 0
+
+    lax.fori_loop(1, count, begin, 0)
+    fall = jnp.exp(-rate[...])
+    states[...] = jnp.zeros_like(states)
+    next_edge[...] = jnp.zeros_like(next_edge)
+
+    def add_a(src, _):
+        pltpu.make_async_remote_copy(
+            src_ref=totals.at[pl.ds(0, order)], dst_ref=held_a.at[src],
+            send_sem=send_a.at[0], recv_sem=recv_a.at[src],
+            device_id={"ctx": lax.rem(me + 1, count)}, device_id_type=MESH,
+        ).wait_recv()
+        states[0:order, :] = fall * states[0:order, :] + held_a[src]
+        return 0
+
+    def add_b(i, _):
+        src = count - 1 - i
+        pltpu.make_async_remote_copy(
+            src_ref=totals.at[pl.ds(order, order)], dst_ref=held_b.at[src],
+            send_sem=send_b.at[0], recv_sem=recv_b.at[src],
+            device_id={"ctx": lax.rem(me + 1, count)}, device_id_type=MESH,
+        ).wait_recv()
+        states[order : 2 * order, :] = fall * states[order : 2 * order, :] + held_b[src]
+        return 0
+
+    lax.fori_loop(0, me, add_a, 0)
+    lax.fori_loop(0, count - 1 - me, add_b, 0)
+
+    @pl.when(me < count - 1)
+    def _():
+        rim().wait_recv()
+        next_edge[...] = held_e[...]
+
+    @pl.when(me >= 1)
+    def _():
+        rim().wait_send()
+
+    def finish(k, _):
+        @pl.when(me + k < count)
+        def _():
+            later(k).wait_send()
+
+        @pl.when(me >= k)
+        def _():
+            earlier(k).wait_send()
+
+        return 0
+
+    lax.fori_loop(1, count, finish, 0)
+
+
+def exchange(totals, edge, span_rate):
     count = lax.axis_size("ctx")
-    result, width = first, 1
-    window = total + jnp.exp(-span_rate) * first
-    reach = 2
-    while width < count - 1:
-        moved = shifted(window, sign * reach)
-        result = result + jnp.exp(-span_rate * float(width)) * moved
-        width += reach
-        if width < count - 1:
-            window = window + jnp.exp(-span_rate * float(reach)) * moved
-        reach *= 2
-    return result
+    order, chans = span_rate.shape
+    dma = pltpu.SemaphoreType.DMA
+    vmem = pl.BlockSpec(memory_space=pltpu.VMEM)
+    return pl.pallas_call(
+        lambda *refs: exchange_kernel(count, *refs),
+        in_specs=[vmem] * 3,
+        out_specs=[vmem] * 2,
+        out_shape=[
+            jax.ShapeDtypeStruct(totals.shape, F32),
+            jax.ShapeDtypeStruct(edge.shape, F32),
+        ],
+        scratch_shapes=[pltpu.VMEM((count, order, chans), F32)] * 2
+        + [pltpu.VMEM(edge.shape, F32)]
+        + [dma((count,))] * 4
+        + [dma((2,))],
+        compiler_params=pltpu.CompilerParams(
+            collective_id=0, has_side_effects=True, vmem_limit_bytes=32 * 2**20
+        ),
+    )(totals, edge, span_rate)
+
+
+def total_kernel(dp_count, ctx_count, parts, result, held, totals, out_1, out_2, in_1, in_2):
+    count = dp_count * ctx_count
+    tiles = parts.shape[0]
+    me = lax.axis_index("dp") * ctx_count + lax.axis_index("ctx")
+    barrier = pltpu.get_barrier_semaphore()
+
+    def place(rank):
+        return {"dp": rank // ctx_count, "ctx": lax.rem(rank, ctx_count)}
+
+    def when(always, cond, run):
+        if always:
+            run()
+        else:
+            pl.when(cond)(run)
+
+    every = count == tiles
+
+    def greet(k, _):
+        pl.semaphore_signal(
+            barrier, inc=1, device_id=place(lax.rem(me + k, count)), device_id_type=MESH
+        )
+        return 0
+
+    lax.fori_loop(1, count, greet, 0)
+    pl.semaphore_wait(barrier, count - 1)
+
+    def part_copy(k, peer, source):
+        return pltpu.make_async_remote_copy(
+            src_ref=parts.at[peer], dst_ref=held.at[source],
+            send_sem=out_1.at[k], recv_sem=in_1.at[source],
+            device_id=place(lax.rem(me + k, count)), device_id_type=MESH,
+        )
+
+    def total_copy(k, source):
+        return pltpu.make_async_remote_copy(
+            src_ref=totals.at[source], dst_ref=totals.at[source],
+            send_sem=out_2.at[k], recv_sem=in_2.at[source],
+            device_id=place(lax.rem(me + k, count)), device_id_type=MESH,
+        )
+
+    def send_part(k, _):
+        peer = lax.rem(me + k, count)
+        when(every, peer < tiles, lambda: part_copy(k, peer, me).start())
+        return 0
+
+    lax.fori_loop(1, count, send_part, 0)
+
+    def own():
+        held[me] = parts[me]
+
+        def arrive(k, _):
+            part_copy(1, 0, lax.rem(me + k, count)).wait_recv()
+            return 0
+
+        lax.fori_loop(1, count, arrive, 0)
+
+        def add(i, acc):
+            return acc + held[i]
+
+        totals[me] = lax.fori_loop(1, count, add, held[0])
+
+        def send_total(k, _):
+            total_copy(k, me).start()
+            return 0
+
+        lax.fori_loop(1, count, send_total, 0)
+
+    when(every, me < tiles, own)
+
+    def got(t, _):
+        @pl.when(t != me)
+        def _():
+            total_copy(1, t).wait_recv()
+
+        return 0
+
+    lax.fori_loop(0, tiles, got, 0)
+    result[...] = totals[...]
+
+    def sent(k, _):
+        peer = lax.rem(me + k, count)
+        when(every, peer < tiles, lambda: part_copy(k, peer, me).wait_send())
+        when(every, me < tiles, lambda: total_copy(k, me).wait_send())
+        return 0
+
+    lax.fori_loop(1, count, sent, 0)
+
+
+def sum_all(parts):
+    dp_count, ctx_count = lax.axis_size("dp"), lax.axis_size("ctx")
+    count = dp_count * ctx_count
+    if count < parts.shape[0]:
+        return lax.psum(parts, ("dp", "ctx"))
+    dma = pltpu.SemaphoreType.DMA
+    vmem = pl.BlockSpec(memory_space=pltpu.VMEM)
+    return pl.pallas_call(
+        lambda *refs: total_kernel(dp_count, ctx_count, *refs),
+        in_specs=[vmem],
+        out_specs=vmem,
+        out_shape=jax.ShapeDtypeStruct(parts.shape, F32),
+        scratch_shapes=[
+            pltpu.VMEM((count,) + parts.shape[1:], F32),
+            pltpu.VMEM(parts.shape, F32),
+            dma((count,)),
+            dma((count,)),
+            dma((count,)),
+            dma((parts.shape[0],)),
+        ],
+        compiler_params=pltpu.CompilerParams(
+            collective_id=1, has_side_effects=True, vmem_limit_bytes=32 * 2**20
+        ),
+    )(parts)
 
 
 def on_device(projected, cotangent, short_filter, residues, decay_rate, skip_gain):
@@ -306,18 +532,7 @@
         ),
     )(proj, cot, rim, taps, rate, perm)
 
-    span_rate = rate * float(tokens)
-    ahead, back = totals[:order], totals[order:]
-    first_ahead = shifted(ahead, 1)
-    first_back = shifted(jnp.concatenate([back, edge], axis=0), -1)
-    next_edge = first_back[order:]
-    states = jnp.concatenate(
-        [
-            entering(ahead, span_rate, first_ahead, 1),
-            entering(back, span_rate, first_back[:order], -1),
-        ],
-        axis=0,
-    )
+    states, next_edge = exchange(totals, edge, rate * float(tokens))
 
     out, grad_in, sums = pl.pallas_call(
         lambda *refs: second_kernel(scale, *refs),
@@ -337,12 +552,12 @@
         out_specs=[
             pl.BlockSpec((LANES, tokens), lambda i: (i, 0)),
             chan_rows(3, tokens),
-            cols(order + SUBS),
+            pl.BlockSpec((None, order + SUBS, LANES), lambda i: (i, 0, 0)),
         ],
         out_shape=[
             jax.ShapeDtypeStruct((chans, tokens), BF16),
             jax.ShapeDtypeStruct((3, chans, tokens), BF16),
-            jax.ShapeDtypeStruct((order + SUBS, chans), F32),
+            jax.ShapeDtypeStruct((tiles, order + SUBS, LANES), F32),
         ],
         scratch_shapes=[pltpu.VMEM((tokens, LANES), F32)] * 4
         + [pltpu.VMEM((order * SUBS, LANES), F32)] * 2
@@ -352,8 +567,9 @@
             flops=12 * work, bytes_accessed=2**23, transcendentals=0
         ),
     )(feat, inner, states, next_edge, taps, rate, res, gain, perm_t, ident)
-    sums = lax.psum(sums, ("dp", "ctx"))
-    return (out[None], grad_in[None], sums[:order].T, sums[order])
+    sums = sum_all(sums)
+    modes = jnp.swapaxes(sums[:, :order], 1, 2).reshape(chans, order)
+    return (out[None], grad_in[None], modes, sums[:, order].reshape(chans))
 
 
 def solution(mesh):

time: 197 us -> 98.5 us (0.50)
  waiting for transfers between devices: 99.1 us -> 2.29 us
  Pallas kernels: 49.4 us -> 74.2 us
  between operations: 14.2 us -> 0.74 us
  starting transfers between devices: 19.6 us -> 7.5 us
    psum x1 -> x0, waiting for transfers between devices: 89.1 us -> none  [on_device(): sums = lax.psum(sums, ('dp', 'ctx'))]
    pallas_call x0 -> x2, Pallas kernels: none -> 25 us  [the longest x1 15.4 us: sum_all(): pl.pallas_call(lambda *refs: total_kernel(dp_count, ctx_count, *refs), in...]
    ppermute x5 -> x1, starting transfers between devices: 15.1 us -> 2.95 us  [shifted(): return lax.ppermute(array, 'ctx', pairs)]
    ppermute x5 -> x1, waiting for transfers between devices: 6.49 us -> 0.01 us  [shifted(): return lax.ppermute(array, 'ctx', pairs)]
  transfers between devices with their start and end apart: 7 -> 2, of which waited for: 5 -> 1; matrix products, arithmetic and copies ran while one was open for 4% -> 10% of each run, Pallas kernels for 0% -> 0%
where the time goes in v1:
time: 98.5 us; the launch traced here: 97.7 us
  Pallas kernels  74.2 us (75%)
  local copies, waits for them, and re-layouts  9.55 us (10%)
  starting transfers between devices  7.5 us (8%)
  other arithmetic  3.44 us (3%)
  waiting for transfers between devices  2.29 us (2%)
    pallas_call x1, Pallas kernels, on_device(): pl.pallas_call(lambda *refs: second_kernel(scale, *refs), grid=(tiles,),...  34.4 us
    pallas_call x1, Pallas kernels, sum_all(): pl.pallas_call(lambda *refs: total_kernel(dp_count, ctx_count, *refs), in...  15.4 us
    pallas_call x1, Pallas kernels, on_device(): pl.pallas_call(first_kernel, grid=(tiles,), in_specs=[chan_rows(3, tokens...  14.8 us
    pallas_call x1, Pallas kernels, exchange(): pl.pallas_call(lambda *refs: exchange_kernel(count, *refs), in_specs=[vme...  9.63 us
    transpose x2, local copies, waits for them, and re-layouts, on_device(): rim = jnp.swapaxes(proj[:, :, tokens - 2:], 1, 2).reshape(6, chans)  4.92 us
    all_to_all x1, starting transfers between devices, on_device(): cot = lax.all_to_all(cot, 'tp', split_axis=0, concat_axis=0, tiled=True)  4.55 us
    ppermute x1, starting transfers between devices, shifted(): return lax.ppermute(array, 'ctx', pairs)  2.95 us
    all_to_all x1, waiting for transfers between devices, on_device(): cot = lax.all_to_all(cot, 'tp', split_axis=0, concat_axis=0, tiled=True)  2.29 us
  transfers between devices with their start and end apart: 2, of which 1 were waited for; matrix products, arithmetic and copies ran while one was open for 10% of the time, Pallas kernels for 0%

profile of v1, /device:TPU:0, one launch (start us, length us, event | category | flops | bytes accessed | tf_op | source)
XLA Modules:
  0.0 97.7 jit_solution(7870954115214829021)
XLA Ops:
  0.6 4.5 %all-to-all-start = ((bf16[2,2048,128]{2,1,0:T(8,128)(2,1)}), bf16[2,2048,128]{2,1,0:T(8,128)(2,1)}, u32[]{:S(2)}, u32[]{:S(2)}) async-start(bf16[2,2048,128]{2,1,0:T(8,128)(2,1)} %bitcast.23), calls=%async_computation | async-start | bytes 2097152 | tf_op jit(solution)/shard_map/all_to_all | solution.py:483
  5.2 0.0 copy-start
  5.2 3.2 %slice_bitcast_fusion = bf16[3,2,2048]{1,2,0:T(8,128)(2,1)} fusion(bf16[3,2048,256]{2,1,0:T(8,128)(2,1)} %bitcast.17), kind=kLoop, calls=%fused_computation | loop fusion | bytes 49152 | tf_op jit(solution)/shard_map/transpose | solution.py:484
  8.4 1.7 %copy.11 = bf16[3,2,2048]{2,1,0:T(2,128)(2,1)S(1)} copy(bf16[3,2,2048]{1,2,0:T(8,128)(2,1)} %slice_bitcast_fusion) | data formatting | bytes 49152 | tf_op jit(solution)/shard_map/transpose | solution.py:484
  10.1 0.0 copy-start.7
  10.1 0.6 reshape.39
  10.8 3.0 %collective-permute-start = (bf16[6,2048]{1,0:T(8,128)(2,1)}, bf16[6,2048]{1,0:T(8,128)(2,1)}, u32[]{:S(2)}, u32[]{:S(2)}) collective-permute-start(bf16[6,2048]{1,0:T(8,128)(2,1)} %reshape.39), channel_id=1, source_target_pairs={{0,2},{2,4},{4,6},{1,3},{3,5},{5,7},{8,10},{10,12},{12,14},{9,11},... | collective-permute-start | bytes 73736 | tf_op jit(solution)/shard_map/ppermute | solution.py:228
  13.7 0.8 fusion.1
  14.5 0.0 copy-done.1
  14.5 0.7 broadcast_multiply_fusion.refs_2_
  15.2 0.6 fusion.2.refs_9_
  15.8 0.9 reshape.40.taps.refs_4_
  16.7 0.0 collective-permute-done
  16.7 1.4 %convert_element_type.12.rim = f32[6,2048]{1,0:T(8,128)} convert(bf16[6,2048]{1,0:T(8,128)(2,1)} %collective-permute-done) | non-fusion elementwise | flops 12288 | bytes 73728 | tf_op jit(solution)/shard_map/convert_element_type | solution.py:485
  18.1 2.3 %all-to-all-done.cot = bf16[2,2048,128]{2,1,0:T(8,128)(2,1)} async-done(((bf16[2,2048,128]{2,1,0:T(8,128)(2,1)}), bf16[2,2048,128]{2,1,0:T(8,128)(2,1)}, u32[]{:S(2)}, u32[]{:S(2)}) %all-to-all-start) | async-done | bytes 1048608 | tf_op jit(solution)/shard_map/all_to_all | solution.py:483
  20.4 0.9 copy-done.3
  21.3 0.8 copy-done.4
  22.2 14.8 %shard_map.93 = (bf16[4,256,2048]{2,1,0:T(8,128)(2,1)S(1)}, f32[256,2048]{1,0:T(8,128)S(1)}, f32[32,2048]{1,0:T(8,128)S(1)}, f32[8,2048]{1,0:T(8,128)S(1)}) custom-call(bf16[3,2048,256]{2,1,0:T(8,128)(2,1)S(1)} %bitcast.18, bf16[2,2048,128]{2,1,0:T(8,128)(2,1)} %all-to-all-done.cot, f32[6,2048]{1,0:T(8,128)S(1)} %copy-done.4, ...), custom_call_target="tpu_custom_call" | custom-call | flops 33554432 | bytes 8388608 | tf_op jit(solution)/shard_map/pallas_call | solution.py:510
  37.0 9.6 %shard_map.94 = (f32[32,2048]{1,0:T(8,128)S(1)}, f32[8,2048]{1,0:T(8,128)S(1)}) custom-call(f32[32,2048]{1,0:T(8,128)S(1)} %get-tuple-element.15.refs_0_, f32[8,2048]{1,0:T(8,128)S(1)} %get-tuple-element.16.refs_1_, f32[16,2048]{1,0:T(8,128)S(1)} %copy-done.2), custom_call_target="tpu_custom_call" | custom-call | tf_op jit(solution)/shard_map/pallas_call | solution.py:340
  46.6 0.0 copy-done.7
  46.6 34.4 %shard_map.95 = (bf16[2048,256]{1,0:T(8,128)(2,1)}, bf16[3,2048,256]{2,1,0:T(8,128)(2,1)}, f32[16,24,128]{2,1,0:T(8,128)S(1)}) custom-call(bf16[4,256,2048]{2,1,0:T(8,128)(2,1)S(1)} %get-tuple-element.13.refs_0_, f32[256,2048]{1,0:T(8,128)S(1)} %get-tuple-element.14.refs_1_, f32[32,2048]{1,0:T(8,128)S(1)} %get-tuple-element.17.refs_2_, ...), custom_call_target="tpu_custom_call" | custom-call | flops 100663296 | bytes 8388608 | tf_op jit(solution)/shard_map/pallas_call | solution.py:537
  81.1 15.4 %shard_map.96 = f32[16,24,128]{2,1,0:T(8,128)S(1)} custom-call(f32[16,24,128]{2,1,0:T(8,128)S(1)} %get-tuple-element.21.refs_0_), custom_call_target="tpu_custom_call" | custom-call | tf_op jit(solution)/shard_map/pallas_call | solution.py:453
  96.4 0.6 slice.11
  97.0 0.7 copy_bitcast_fusion
  (11 shorter events, 0.0 us)
Async XLA Ops:
  0.6 13.9 %copy-start.1 = (f32[2048,16]{0,1:T(8,128)S(1)}, f32[2048,16]{0,1:T(8,128)}, u32[]{:S(2)}) copy-start(f32[2048,16]{0,1:T(8,128)} %param.10) | copy-start | bytes 393220
  0.6 19.8 %all-to-all-start = ((bf16[2,2048,128]{2,1,0:T(8,128)(2,1)}), bf16[2,2048,128]{2,1,0:T(8,128)(2,1)}, u32[]{:S(2)}, u32[]{:S(2)}) async-start(bf16[2,2048,128]{2,1,0:T(8,128)(2,1)} %bitcast.23), calls=%async_computation | async-start | bytes 2097152 | tf_op jit(solution)/shard_map/all_to_all | solution.py:483
  5.2 15.2 %copy-start = (bf16[1,3,2048,256]{3,2,1,0:T(8,128)(2,1)S(1)}, bf16[1,3,2048,256]{3,2,1,0:T(8,128)(2,1)}, u32[]{:S(2)}) copy-start(bf16[1,3,2048,256]{3,2,1,0:T(8,128)(2,1)} %param.6) | copy-start | bytes 9437188
  10.1 36.5 %copy-start.7 = (f32[2048]{0:T(1024)S(1)}, f32[2048]{0:T(1024)}, u32[]{:S(2)}) copy-start(f32[2048]{0:T(1024)} %param.11) | copy-start | bytes 24580
  10.8 5.9 %collective-permute-start = (bf16[6,2048]{1,0:T(8,128)(2,1)}, bf16[6,2048]{1,0:T(8,128)(2,1)}, u32[]{:S(2)}, u32[]{:S(2)}) collective-permute-start(bf16[6,2048]{1,0:T(8,128)(2,1)} %reshape.39), channel_id=1, source_target_pairs={{0,2},{2,4},{4,6},{1,3},{3,5},{5,7},{8,10},{10,12},{12,14},{9,11},... | collective-permute-start | bytes 73736 | tf_op jit(solution)/shard_map/ppermute | solution.py:228
  20.4 16.6 %copy-start.2 = (f32[16,2048]{1,0:T(8,128)S(1)}, f32[16,2048]{1,0:T(8,128)}, u32[]{:S(2)}) copy-start(f32[16,2048]{1,0:T(8,128)} %broadcast_multiply_fusion.refs_2_) | copy-start | bytes 393220
  20.4 0.9 copy-start.3
  21.3 0.8 copy-start.4
  22.2 24.4 %copy-start.5 = (f32[2048,16]{0,1:T(8,128)S(1)}, f32[2048,16]{0,1:T(8,128)}, u32[]{:S(2)}) copy-start(f32[2048,16]{0,1:T(8,128)} %param.9) | copy-start | bytes 393220
  22.2 24.4 %copy-start.6 = (bf16[128,128]{1,0:T(8,128)(2,1)S(1)}, bf16[128,128]{1,0:T(8,128)(2,1)}, u32[]{:S(2)}) copy-start(bf16[128,128]{1,0:T(8,128)(2,1)} %fusion.2.refs_9_) | copy-start | bytes 98308

commit v2 on v1

--- a/solution.py
+++ b/solution.py
@@ -2,6 +2,7 @@
 
 import jax
 import jax.numpy as jnp
+import numpy as np
 from jax import lax
 from jax.experimental import pallas as pl
 from jax.experimental.pallas import tpu as pltpu
@@ -9,6 +10,7 @@
 
 LANES = 128
 SUBS = 8
+FOLD = 4
 F32 = jnp.float32
 BF16 = jnp.bfloat16
 
@@ -54,6 +56,36 @@
     else:
         before = jnp.where(sub >= 1, pltpu.roll(running, 1, 0), 0.0)
     return before, running
+
+
+def folded(kernel, fold, axes):
+    def run(*refs):
+        for h in range(fold):
+            views = []
+            for ref, axis in zip(refs, axes):
+                if axis is None:
+                    views.append(ref)
+                elif axis == "tile":
+                    views.append(ref.at[h])
+                else:
+                    where = [slice(None)] * len(ref.shape)
+                    where[axis] = pl.ds(h * LANES, LANES)
+                    views.append(ref.at[tuple(where)])
+            kernel(*views, *refs[len(axes) :])
+
+    return run
+
+
+def rim_kernel(proj, rim):
+    width = proj.shape[2]
+    row = lax.broadcasted_iota(jnp.int32, (SUBS, width), 0)
+    column = lax.broadcasted_iota(jnp.int32, (SUBS, width), 1)
+    total = None
+    for s in range(3):
+        pick = jnp.where((row // 2 == s) & (column == width - 2 + row % 2), 1.0, 0.0)
+        part = nt_dot(pick.astype(BF16), proj[s])
+        total = part if total is None else total + part
+    rim[...] = total
 
 
 def first_kernel(proj, cot, rim, taps, rate, perm, feat, inner, totals, edge, u_s, d_s):
@@ -481,39 +513,52 @@
 
     cot = cotangent[0].reshape(pieces, chans, tokens // pieces)
     cot = lax.all_to_all(cot, "tp", split_axis=0, concat_axis=0, tiled=True)
-    rim = jnp.swapaxes(proj[:, :, tokens - 2 :], 1, 2).reshape(6, chans)
-    rim = shifted(rim, 1).astype(F32)
+    last_lanes = math.gcd(tokens, LANES)
+    rim = pl.pallas_call(
+        rim_kernel,
+        grid=(1,),
+        in_specs=[
+            pl.BlockSpec((3, chans, last_lanes), lambda i: (0, 0, tokens // last_lanes - 1))
+        ],
+        out_specs=pl.BlockSpec((SUBS, chans), lambda i: (0, 0)),
+        out_shape=jax.ShapeDtypeStruct((SUBS, chans), F32),
+        compiler_params=pltpu.CompilerParams(vmem_limit_bytes=24 * 2**20),
+        cost_estimate=pl.CostEstimate(flops=2**24, bytes_accessed=2**21, transcendentals=0),
+    )(proj)
+    rim = shifted(rim, 1)
     taps = short_filter.reshape(9, chans)
     rate = decay_rate.T
     res = residues.T
     gain = skip_gain[None]
-    r = jnp.arange(tokens)
-    perm = ((r % SUBS) * span + r // SUBS)[:, None] == r[None, :]
-    perm_t = perm.T.astype(BF16)
-    perm = perm.astype(BF16)
-    ident = jnp.eye(LANES, dtype=BF16)
+    r = np.arange(tokens)
+    order_of = ((r % SUBS) * span + r // SUBS)[:, None] == r[None, :]
+    perm = jnp.asarray(order_of.astype(BF16))
+    perm_t = jnp.asarray(order_of.T.astype(BF16))
+    ident = jnp.asarray(np.eye(LANES).astype(BF16))
+    fold = math.gcd(FOLD, tiles)
+    block = fold * LANES
 
     def cols(*lead):
         zeros = (0,) * len(lead)
-        return pl.BlockSpec(lead + (LANES,), lambda i: zeros + (i,))
+        return pl.BlockSpec(lead + (block,), lambda i: zeros + (i,))
 
     def whole(rows, columns):
         return pl.BlockSpec((rows, columns), lambda i: (0, 0))
 
     def chan_rows(lead, last):
-        return pl.BlockSpec((lead, LANES, last), lambda i: (0, i, 0))
+        return pl.BlockSpec((lead, block, last), lambda i: (0, i, 0))
 
     params = pltpu.CompilerParams(
         dimension_semantics=("arbitrary",), vmem_limit_bytes=40 * 2**20
     )
     work = chans * tokens * order
     feat, inner, totals, edge = pl.pallas_call(
-        first_kernel,
-        grid=(tiles,),
+        folded(first_kernel, fold, [1, 1, 1, 1, 1, None, 2, 1, 1, 1]),
+        grid=(tiles // fold,),
         in_specs=[
             chan_rows(3, tokens),
             chan_rows(pieces, tokens // pieces),
-            cols(6),
+            cols(SUBS),
             cols(9),
             cols(order),
             whole(tokens, tokens),
@@ -535,8 +580,12 @@
     states, next_edge = exchange(totals, edge, rate * float(tokens))
 
     out, grad_in, sums = pl.pallas_call(
-        lambda *refs: second_kernel(scale, *refs),
-        grid=(tiles,),
+        folded(
+            lambda *refs: second_kernel(scale, *refs),
+            fold,
+            [2, 1, 1, 1, 1, 1, 1, 1, None, None, 0, 1, "tile"],
+        ),
+        grid=(tiles // fold,),
         in_specs=[
             cols(4, tokens),
             cols(2 * order * SUBS),
@@ -550,9 +599,9 @@
             whole(LANES, LANES),
         ],
         out_specs=[
-            pl.BlockSpec((LANES, tokens), lambda i: (i, 0)),
+            pl.BlockSpec((block, tokens), lambda i: (i, 0)),
             chan_rows(3, tokens),
-            pl.BlockSpec((None, order + SUBS, LANES), lambda i: (i, 0, 0)),
+            pl.BlockSpec((fold, order + SUBS, LANES), lambda i: (i, 0, 0)),
         ],
         out_shape=[
             jax.ShapeDtypeStruct((chans, tokens), BF16),

time: 98.5 us -> 93.6 us (0.950)
  waiting for transfers between devices: 2.29 us -> 8 us
  local copies, waits for them, and re-layouts: 9.55 us -> 5.05 us
  other arithmetic: 3.44 us -> 0.01 us
  Pallas kernels: 74.2 us -> 71.8 us
    all_to_all x1, waiting for transfers between devices: 2.29 us -> 8 us  [on_device(): cot = lax.all_to_all(cot, 'tp', split_axis=0, concat_axis=0, tiled=True)]
    transpose x2 -> x0, local copies, waits for them, and re-layouts: 4.92 us -> none  [on_device(): rim = jnp.swapaxes(proj[:, :, tokens - 2:], 1, 2).reshape(6, chans)]
    convert_element_type x3 -> x0, other arithmetic: 2.76 us -> none  [the longest x1 1.39 us: on_device(): rim = shifted(rim, 1).astype(F32)]
    pallas_call x2 -> x3, Pallas kernels: 49.2 us -> 46.8 us  [the longest x1 32.6 us: on_device(): pl.pallas_call(folded(lambda *refs: second_kernel(scale, *refs), fold, [2...]
    unnamed x16, local copies, waits for them, and re-layouts: 1.81 us -> 2.85 us
  transfers between devices with their start and end apart: 2 -> 2, of which waited for: 1 -> 1; matrix products, arithmetic and copies ran while one was open for 10% -> 1% of each run, Pallas kernels for 0% -> 1%
where the time goes in v2:
time: 93.6 us; the launch traced here: 93.2 us
  Pallas kernels  71.8 us (77%)
  waiting for transfers between devices  8 us (9%)
  starting transfers between devices  7.66 us (8%)
  local copies, waits for them, and re-layouts  5.05 us (5%)
    pallas_call x1, Pallas kernels, on_device(): pl.pallas_call(folded(lambda *refs: second_kernel(scale, *refs), fold, [2...  32.6 us
    pallas_call x1, Pallas kernels, sum_all(): pl.pallas_call(lambda *refs: total_kernel(dp_count, ctx_count, *refs), in...  15.4 us
    pallas_call x1, Pallas kernels, on_device(): pl.pallas_call(folded(first_kernel, fold, [1, 1, 1, 1, 1, None, 2, 1, 1,...  13 us
    pallas_call x1, Pallas kernels, exchange(): pl.pallas_call(lambda *refs: exchange_kernel(count, *refs), in_specs=[vme...  9.65 us
    all_to_all x1, waiting for transfers between devices, on_device(): cot = lax.all_to_all(cot, 'tp', split_axis=0, concat_axis=0, tiled=True)  8 us
    all_to_all x1, starting transfers between devices, on_device(): cot = lax.all_to_all(cot, 'tp', split_axis=0, concat_axis=0, tiled=True)  4.55 us
    ppermute x1, starting transfers between devices, shifted(): return lax.ppermute(array, 'ctx', pairs)  3.11 us
    unnamed x16, local copies, waits for them, and re-layouts  2.85 us
  transfers between devices with their start and end apart: 2, of which 1 were waited for; matrix products, arithmetic and copies ran while one was open for 1% of the time, Pallas kernels for 1%

profile of v2, /device:TPU:0, one launch (start us, length us, event | category | flops | bytes accessed | tf_op | source)
XLA Modules:
  0.0 93.2 jit_solution(188146198935404264)
XLA Ops:
  0.6 0.0 copy-start.2
  0.6 4.6 %all-to-all-start = ((bf16[2,2048,128]{2,1,0:T(8,128)(2,1)}), bf16[2,2048,128]{2,1,0:T(8,128)(2,1)}, u32[]{:S(2)}, u32[]{:S(2)}) async-start(bf16[2,2048,128]{2,1,0:T(8,128)(2,1)} %bitcast.21), calls=%async_computation | async-start | bytes 2097152 | tf_op jit(solution)/shard_map/all_to_all | solution.py:515
  5.2 0.0 copy-start
  5.2 1.9 %copy-done = bf16[1,3,2048,256]{3,2,1,0:T(8,128)(2,1)S(1)} copy-done((bf16[1,3,2048,256]{3,2,1,0:T(8,128)(2,1)S(1)}, bf16[1,3,2048,256]{3,2,1,0:T(8,128)(2,1)}, u32[]{:S(2)}) %copy-start) | copy-done | bytes 3145752
  7.1 0.0 copy-start.1
  7.1 1.2 %shard_map.120 = f32[8,2048]{1,0:T(8,128)} custom-call(bf16[3,2048,256]{2,1,0:T(8,128)(2,1)S(1)} %bitcast.15), custom_call_target="tpu_custom_call" | custom-call | flops 16777216 | bytes 2097152 | tf_op jit(solution)/shard_map/pallas_call | solution.py:517
  8.3 0.0 copy-start.7
  8.3 3.1 %collective-permute-start = (f32[8,2048]{1,0:T(8,128)}, f32[8,2048]{1,0:T(8,128)}, u32[]{:S(2)}, u32[]{:S(2)}) collective-permute-start(f32[8,2048]{1,0:T(8,128)} %shard_map.120), channel_id=1, source_target_pairs={{0,2},{2,4},{4,6},{1,3},{3,5},{5,7},{8,10},{10,12},{12,14},{9,11},... | collective-permute-start | bytes 196616 | tf_op jit(solution)/shard_map/ppermute | solution.py:260
  11.4 0.0 copy-done.2
  11.4 0.9 %reshape.14.refs_3_.refs_4_ = f32[9,2048]{1,0:T(8,128)S(1)} reshape(f32[3,3,2048]{2,1,0:T(4,128)} %param.11) | data formatting | bytes 147456 | tf_op jit(solution)/shard_map/reshape | solution.py:529
  12.4 0.0 collective-permute-done.refs_2_
  12.4 8.0 %all-to-all-done.refs_1_ = bf16[2,2048,128]{2,1,0:T(8,128)(2,1)} async-done(((bf16[2,2048,128]{2,1,0:T(8,128)(2,1)}), bf16[2,2048,128]{2,1,0:T(8,128)(2,1)}, u32[]{:S(2)}, u32[]{:S(2)}) %all-to-all-start) | async-done | bytes 1048608 | tf_op jit(solution)/shard_map/all_to_all | solution.py:515
  20.4 0.0 copy-done.1
  20.4 0.9 %copy-done.5 = bf16[256,256]{1,0:T(8,128)(2,1)S(1)} copy-done((bf16[256,256]{1,0:T(8,128)(2,1)S(1)}, bf16[256,256]{1,0:T(8,128)(2,1)}, u32[]{:S(2)}) %copy-start.5) | copy-done | bytes 131096
  21.3 13.0 %shard_map.121 = (bf16[4,256,2048]{2,1,0:T(8,128)(2,1)S(1)}, f32[256,2048]{1,0:T(8,128)S(1)}, f32[32,2048]{1,0:T(8,128)S(1)}, f32[8,2048]{1,0:T(8,128)S(1)}) custom-call(bf16[3,2048,256]{2,1,0:T(8,128)(2,1)S(1)} %bitcast.16, bf16[2,2048,128]{2,1,0:T(8,128)(2,1)} %all-to-all-done.refs_1_, f32[8,2048]{1,0:T(8,128)} %collective-permute-done.refs_2_, ...), custom_call_target="tpu_custom_call" | custom-call | flops 33554432 | bytes 8388608 | tf_op jit(solution)/shard_map/pallas_call | solution.py:555
  34.3 9.7 %shard_map.122 = (f32[32,2048]{1,0:T(8,128)S(1)}, f32[8,2048]{1,0:T(8,128)S(1)}) custom-call(f32[32,2048]{1,0:T(8,128)S(1)} %get-tuple-element.15.refs_0_, f32[8,2048]{1,0:T(8,128)S(1)} %get-tuple-element.16.refs_1_, f32[16,2048]{1,0:T(8,128)S(1)} %broadcast_multiply_fusion.refs_2_), custom_call_target="tpu_custom_call" | custom-call | tf_op jit(solution)/shard_map/pallas_call | solution.py:372
  44.0 0.0 copy-done.7
  44.0 0.0 copy-done.3
  44.0 0.0 copy-done.4
  44.0 0.0 copy-done.6
  44.0 32.6 %shard_map.123 = (bf16[2048,256]{1,0:T(8,128)(2,1)}, bf16[3,2048,256]{2,1,0:T(8,128)(2,1)}, f32[16,24,128]{2,1,0:T(8,128)S(1)}) custom-call(bf16[4,256,2048]{2,1,0:T(8,128)(2,1)S(1)} %get-tuple-element.13.refs_0_, f32[256,2048]{1,0:T(8,128)S(1)} %get-tuple-element.14.refs_1_, f32[32,2048]{1,0:T(8,128)S(1)} %get-tuple-element.17.refs_2_, ...), custom_call_target="tpu_custom_call" | custom-call | flops 100663296 | bytes 8388608 | tf_op jit(solution)/shard_map/pallas_call | solution.py:582
  76.6 15.4 %shard_map.124 = f32[16,24,128]{2,1,0:T(8,128)S(1)} custom-call(f32[16,24,128]{2,1,0:T(8,128)S(1)} %get-tuple-element.21.refs_0_), custom_call_target="tpu_custom_call" | custom-call | tf_op jit(solution)/shard_map/pallas_call | solution.py:485
  92.0 0.6 slice.7
  92.6 0.7 copy_bitcast_fusion
  (5 shorter events, 0.0 us)
Async XLA Ops:
  0.6 10.8 %copy-start.2 = (f32[2048,16]{0,1:T(8,128)S(1)}, f32[2048,16]{0,1:T(8,128)}, u32[]{:S(2)}) copy-start(f32[2048,16]{0,1:T(8,128)} %param.13) | copy-start | bytes 393220
  0.6 19.7 %all-to-all-start = ((bf16[2,2048,128]{2,1,0:T(8,128)(2,1)}), bf16[2,2048,128]{2,1,0:T(8,128)(2,1)}, u32[]{:S(2)}, u32[]{:S(2)}) async-start(bf16[2,2048,128]{2,1,0:T(8,128)(2,1)} %bitcast.21), calls=%async_computation | async-start | bytes 2097152 | tf_op jit(solution)/shard_map/all_to_all | solution.py:515
  5.2 1.9 %copy-start = (bf16[1,3,2048,256]{3,2,1,0:T(8,128)(2,1)S(1)}, bf16[1,3,2048,256]{3,2,1,0:T(8,128)(2,1)}, u32[]{:S(2)}) copy-start(bf16[1,3,2048,256]{3,2,1,0:T(8,128)(2,1)} %param.9) | copy-start | bytes 9437188
  7.1 13.3 %copy-start.1 = (bf16[1,3,2048,256]{3,2,1,0:T(8,128)(2,1)S(1)}, bf16[1,3,2048,256]{3,2,1,0:T(8,128)(2,1)}, u32[]{:S(2)}) copy-start(bf16[1,3,2048,256]{3,2,1,0:T(8,128)(2,1)} %param.9) | copy-start | bytes 9437188
  8.3 35.7 %copy-start.7 = (f32[2048]{0:T(1024)S(1)}, f32[2048]{0:T(1024)}, u32[]{:S(2)}) copy-start(f32[2048]{0:T(1024)} %param.14) | copy-start | bytes 24580
  8.3 4.1 %collective-permute-start = (f32[8,2048]{1,0:T(8,128)}, f32[8,2048]{1,0:T(8,128)}, u32[]{:S(2)}, u32[]{:S(2)}) collective-permute-start(f32[8,2048]{1,0:T(8,128)} %shard_map.120), channel_id=1, source_target_pairs={{0,2},{2,4},{4,6},{1,3},{3,5},{5,7},{8,10},{10,12},{12,14},{9,11},... | collective-permute-start | bytes 196616 | tf_op jit(solution)/shard_map/ppermute | solution.py:260
  20.4 23.6 %copy-start.3 = (f32[2048,16]{0,1:T(8,128)S(1)}, f32[2048,16]{0,1:T(8,128)}, u32[]{:S(2)}) copy-start(f32[2048,16]{0,1:T(8,128)} %param.12) | copy-start | bytes 393220
  20.4 23.6 %copy-start.4 = (bf16[256,256]{1,0:T(8,128)(2,1)S(1)}, bf16[256,256]{1,0:T(8,128)(2,1)}, u32[]{:S(2)}) copy-start(bf16[256,256]{1,0:T(8,128)(2,1)} %constant.9.clone.refs_8_) | copy-start | bytes 393220
  20.4 0.9 %copy-start.5 = (bf16[256,256]{1,0:T(8,128)(2,1)S(1)}, bf16[256,256]{1,0:T(8,128)(2,1)}, u32[]{:S(2)}) copy-start(bf16[256,256]{1,0:T(8,128)(2,1)} %constant.8.clone.refs_5_) | copy-start | bytes 393220
  21.3 22.7 %copy-start.6 = (bf16[128,128]{1,0:T(8,128)(2,1)S(1)}, bf16[128,128]{1,0:T(8,128)(2,1)}, u32[]{:S(2)}) copy-start(bf16[128,128]{1,0:T(8,128)(2,1)} %constant.10.clone.refs_9_) | copy-start | bytes 98308
